TPU v7x, 512 devices: a whole 4x8x8 slice. The times are simulated.
512 devices in a mesh: row: 16 (over z_hi, x, core), col: 32 (over y, z_lo).
Axes of the slice: x: 4, y: 8, z: 8 (z_hi: 2, z_lo: 4; z = z_hi * 4 + z_lo), core: 2. Of those that a mesh axis runs over, the one named last changes fastest.
Arguments:
- residual: bfloat16 [32768, 1536], P(('row', 'col')), may hold values from -6 to 6
- bins: int32 [32768], P(('row', 'col')), may hold values from 0 to 15
- bin_scale: float32 [16], replicated, may hold values from 0.1 to 1
- blocks: bfloat16 [32768, 12288], P(('row', 'col')), may hold values from -0.4375 to 0.4375
- block_row: int32 [32768], P(('row', 'col')), may hold values from 0 to 2047, as said below
- block_col: int32 [32768], P(('row', 'col')), may hold values from 0 to 7
- counts: int32 [8192], P(('row', 'col')), may hold values from 1 to 4, as said below
Outputs:
- coarse: float32 [32, 128, 512], P('col', 'row')
Inputs may be any that keep to these rules, and one draw needn't show every extreme that they name: `counts`: every device has a bucket with 4 live slots, and in one column group every row group sends 4 live slots to the same aggregate piece. Among the 16 * 4 slots of one device, at most 4 have the same value of block_row // 64, and exactly 4 for some value.
All inputs are finite; a program needn't handle non-finite values.
Results may differ from a plain program's by a relative error of at most 0.00035.
Values may be sent and summed in bfloat16 or wider, within the bound.
A program may use at most 64 MiB of HBM per device.

v0:
```python
import jax
import jax.numpy as jnp
from jax import lax
from jax.sharding import PartitionSpec as P

CASES = 8
AG_DEV = 8


def products(panels, blocks):
    count = panels.shape[0]
    width = blocks.shape[1]
    panel_view = panels.reshape(count, CASES, -1)
    fine_dofs = panel_view.shape[2]
    block_view = blocks.reshape(count, fine_dofs, width // fine_dofs)
    prod = jnp.einsum("ncf,nfa->nca", panel_view, block_view, preferred_element_type=jnp.float32)
    return prod.reshape(count, -1)


def weights_of(bin_ids, live_flag, bin_scale):
    levels = jnp.arange(bin_scale.shape[0], dtype=jnp.int32)
    chosen = jnp.sum(
        jnp.where(bin_ids[:, None] == levels[None, :], bin_scale[None, :], 0.0), axis=1
    )
    return chosen * live_flag.astype(jnp.float32)


def accumulate(terms, targets, number):
    onehot = (targets[None, :] == jnp.arange(number, dtype=jnp.int32)[:, None]).astype(jnp.float32)
    return jnp.dot(
        onehot, terms, precision=lax.Precision.HIGHEST, preferred_element_type=jnp.float32
    )


def shards(residual, bins, bin_scale, blocks, block_row, block_col, counts):
    n_row = lax.axis_size("row")
    total = block_row.shape[0]
    cap = total // n_row
    whole, whole_bins = (
        lax.all_gather(residual, "col", axis=0, tiled=True),
        lax.all_gather(bins, "col", axis=0, tiled=True),
    )
    panels = jnp.take(whole, block_row, axis=0)
    slot_bins = jnp.take(whole_bins, block_row, axis=0)
    place = jnp.arange(total, dtype=jnp.int32) % cap
    live_flag = (place < jnp.repeat(counts, cap)).astype(jnp.int32)
    weight = weights_of(slot_bins, live_flag, bin_scale)
    terms = weight[:, None] * products(panels, blocks)
    moved_terms, moved_cols = (
        lax.all_to_all(terms, "row", split_axis=0, concat_axis=0, tiled=True),
        lax.all_to_all(block_col, "row", split_axis=0, concat_axis=0, tiled=True),
    )
    coarse = accumulate(moved_terms, moved_cols, AG_DEV)
    return coarse[None]


def solution(mesh):
    in_specs = (
        P(("row", "col"), None),
        P(("row", "col")),
        P(),
        P(("row", "col"), None),
        P(("row", "col")),
        P(("row", "col")),
        P(("row", "col")),
    )
    out_specs = P("col", "row", None)
    return jax.shard_map(shards, mesh=mesh, in_specs=in_specs, out_specs=out_specs, check_vma=False)
```

profile of v0, /device:TPU:1, one launch (start us, length us, event | category | flops | bytes accessed | tf_op | source)
XLA Modules:
  0.0 220.1 jit_solution(1076800710245611079)
XLA Ops:
  6.5 0.0 copy-start
  6.5 0.0 all-gather.2.cloned.1.call-start
  6.5 0.7 all-gather.2.cloned.1.call-update
  7.3 1.3 all_to_all.12
  8.6 14.3 %all-to-all-start = ((s32[16,4,1]{1,2,0:T(1,128)}), s32[16,4,1]{1,2,0:T(1,128)S(1)}, u32[]{:S(2)}, u32[]{:S(2)}) async-start(s32[16,4,1]{1,2,0:T(1,128)} %bitcast), calls=%async_computation | async-start | bytes 16384 | tf_op jit(solution)/shard_map/all_to_all | solution.py:51
  22.9 1.3 dynamic-slice
  24.8 0.9 dynamic-update-slice
  25.7 17.6 %all-reduce = s32[2048]{0:T(1024)S(1)} all-reduce(s32[2048]{0:T(1024)S(1)} %dynamic-update-slice), channel_id=1, replica_groups=mesh['row'=16,'col'=32] {'col'}, use_global_device_ids=true, to_apply=%add | all-reduce | flops 2048 | bytes 16384
  43.3 0.7 compare_select_fusion
  44.0 0.8 gather_fusion
  44.7 0.7 broadcast_select_fusion
  45.4 0.7 select_reduce_fusion
  46.1 0.1 reduce_sum.12
  46.2 4.3 %reshape.54 = bf16[64,192,64]{2,1,0:T(8,128)(2,1)S(1)} reshape(bf16[64,12288]{1,0:T(8,128)(2,1)} %param.10) | data formatting | bytes 3145728 | tf_op jit(solution)/shard_map/reshape | solution.py:15
  50.5 0.0 copy-done
  50.6 0.1 convert_multiply_fusion
  50.6 112.3 %all-gather.2.cloned.1.call-done = bf16[2048,1536]{1,0:T(8,128)(2,1)} async-done(((bf16[64,1536]{1,0:T(8,128)(2,1)}), bf16[2048,1536]{1,0:T(8,128)(2,1)}) %all-gather.2.cloned.1.call-update) | async-done | bytes 6291472 | tf_op jit(solution)/shard_map/all_gather | solution.py:40
  162.9 5.2 %gather_fusion.1 = bf16[64,1536]{1,0:T(8,128)(2,1)} fusion(bf16[2048,1536]{1,0:T(8,128)(2,1)} %all-gather.2.cloned.1.call-done, s32[1024]{0:T(1024)S(1)} %pad_clamp_fusion), kind=kCustom, calls=%fused_computation.1 | custom fusion | bytes 393472 | tf_op jit(solution)/shard_map/jit(_take)/gather | solution.py:43
  168.1 1.2 gather.12
  169.2 1.7 fusion
  170.9 1.1 reshape.55
  172.0 0.7 broadcast_multiply_fusion
  172.7 0.0 all-to-all-done
  172.7 29.6 %all-to-all-start.1 = ((f32[16,4,512]{2,1,0:T(4,128)}), f32[16,4,512]{2,1,0:T(4,128)S(1)}, u32[]{:S(2)}, u32[]{:S(2)}) async-start(f32[16,4,512]{2,1,0:T(4,128)} %broadcast_multiply_fusion), calls=%async_computation.1 | async-start | bytes 262144 | tf_op jit(solution)/shard_map/all_to_all | solution.py:50
  202.4 0.5 broadcast.47
  202.9 0.7 reduce.3
  203.6 0.1 eq.30
  203.7 8.8 %all-to-all-done.1 = f32[16,4,512]{2,1,0:T(4,128)S(1)} async-done(((f32[16,4,512]{2,1,0:T(4,128)}), f32[16,4,512]{2,1,0:T(4,128)S(1)}, u32[]{:S(2)}, u32[]{:S(2)}) %all-to-all-start.1) | async-done | bytes 131104 | tf_op jit(solution)/shard_map/all_to_all | solution.py:50
  212.5 0.8 convolution_bitcast_fusion
  (3 shorter events, 0.1 us)
Async XLA Ops:
  6.5 44.0 %copy-start = (s32[16]{0:T(128)S(1)}, s32[16]{0:T(128)}, u32[]{:S(2)}) copy-start(s32[16]{0:T(128)} %param.13) | copy-start | bytes 196
  6.5 156.4 %all-gather.2.cloned.1.call-start = ((), (), s32[]{:S(2)}) async-start(), calls=%async_computation.2 | async-start | bytes 6488064 | tf_op jit(solution)/shard_map/all_gather | solution.py:40
  8.6 164.1 %all-to-all-start = ((s32[16,4,1]{1,2,0:T(1,128)}), s32[16,4,1]{1,2,0:T(1,128)S(1)}, u32[]{:S(2)}, u32[]{:S(2)}) async-start(s32[16,4,1]{1,2,0:T(1,128)} %bitcast), calls=%async_computation | async-start | bytes 16384 | tf_op jit(solution)/shard_map/all_to_all | solution.py:51
  172.7 39.7 %all-to-all-start.1 = ((f32[16,4,512]{2,1,0:T(4,128)}), f32[16,4,512]{2,1,0:T(4,128)S(1)}, u32[]{:S(2)}, u32[]{:S(2)}) async-start(f32[16,4,512]{2,1,0:T(4,128)} %broadcast_multiply_fusion), calls=%async_computation.1 | async-start | bytes 262144 | tf_op jit(solution)/shard_map/all_to_all | solution.py:50
Sparse Core Ops, SparseCore 0:
  9.4 153.4 all-gather.1
where the time goes:
time: 221 us; the launch traced here: 220 us
  waiting for transfers between devices  122 us (55%)
  starting transfers between devices  43.9 us (20%)
  blocking collectives  17.6 us (8%)
  local copies, waits for them, and re-layouts  16.7 us (8%)
  between operations  14.1 us (6%)
  other arithmetic  3.55 us (2%)
  matrix products  2.44 us (1%)
    all_gather x1, waiting for transfers between devices, shards(): lax.all_gather(residual, 'col', axis=0, tiled=True)  112 us
    all_to_all x1, starting transfers between devices, shards(): lax.all_to_all(terms, 'row', split_axis=0, concat_axis=0, tiled=True)  29.6 us
    unnamed x1, blocking collectives  17.6 us
    all_to_all x1, starting transfers between devices, shards(): lax.all_to_all(block_col, 'row', split_axis=0, concat_axis=0, tiled=True)  14.3 us
    all_to_all x1, waiting for transfers between devices, shards(): lax.all_to_all(terms, 'row', split_axis=0, concat_axis=0, tiled=True)  8.78 us
    gather x2, local copies, waits for them, and re-layouts, shards(): panels = jnp.take(whole, block_row, axis=0)  6.33 us
  transfers between devices with their start and end apart: 3, of which 2 were waited for; matrix products, arithmetic and copies ran while one was open for 9% of the time, Pallas kernels for 0%

commit v1 on v0

v1 whole, which is shorter than its diff:
```python
import functools

import jax
import jax.numpy as jnp
from jax import lax
from jax.experimental import pallas as pl
from jax.experimental.pallas import tpu as pltpu
from jax.sharding import PartitionSpec as P

CASES = 8
AG_DEV = 8
REQ = 4
LANES = 128
MESH = pl.DeviceIdType.MESH


def iota(shape, dim):
    return lax.broadcasted_iota(jnp.int32, shape, dim)


def dot(a, b, dims=((1,), (0,))):
    return lax.dot_general(
        a.astype(jnp.bfloat16),
        b.astype(jnp.bfloat16),
        (dims, ((), ())),
        preferred_element_type=jnp.float32,
    )


def wait_bytes(ref, sem):
    pltpu.make_async_copy(ref, ref, sem).wait()


def pair_up(row, pairs):
    shape = (pairs, row.shape[1])
    spread = jnp.broadcast_to(row, shape)
    low = jnp.sum(jnp.where(iota(shape, 1) == 2 * iota(shape, 0), spread, 0.0), axis=1, keepdims=True)
    high = jnp.sum(jnp.where(iota(shape, 1) == 2 * iota(shape, 0) + 1, spread, 0.0), axis=1, keepdims=True)
    wide = (pairs, LANES)
    return jnp.where(iota(wide, 1) < LANES // 2, jnp.broadcast_to(low, wide), jnp.broadcast_to(high, wide))


def kernel(
    n_row,
    n_col,
    residual,
    blocks,
    block_row_at,
    block_col_at,
    bins_at,
    counts_at,
    bin_scale_at,
    coarse,
    block_row,
    block_col,
    bins,
    counts,
    bin_scale,
    padded,
    res,
    blk,
    wide,
    packed,
    table,
    ask,
    asked,
    asked_s,
    place,
    place_s,
    answer,
    got,
    terms,
    summands,
    cols,
    got_cols,
    weights,
    folded,
    load_sem,
    place_sem,
    ask_sem,
    ask_in,
    asked_sem,
    answer_sem,
    answer_in,
    term_sem,
    term_in,
    cols_sem,
    cols_in,
):
    row, col = lax.axis_index("row"), lax.axis_index("col")
    fine_dev, width = res.shape
    slots = blk.shape[0]
    cap = slots // n_row
    dofs = width // CASES
    half = dofs // 2
    groups = 2 * CASES
    tiles = blk.shape[1] // LANES

    small = [
        pltpu.make_async_copy(a, b, load_sem.at[2 + i])
        for i, (a, b) in enumerate(
            (
                (block_row_at, block_row),
                (block_col_at, block_col),
                (bins_at, bins),
                (counts_at, counts),
                (bin_scale_at, bin_scale),
            )
        )
    ]
    for load in small:
        load.start()
    load_res = pltpu.make_async_copy(residual, res, load_sem.at[0])
    load_res.start()
    load_blk = pltpu.make_async_copy(blocks, blk, load_sem.at[1])
    load_blk.start()

    barrier = pltpu.get_barrier_semaphore()

    @pl.loop(1, n_col)
    def _(j):
        pl.semaphore_signal(barrier, inc=1, device_id={"col": lax.rem(col + j, n_col)}, device_id_type=MESH)

    @pl.loop(1, n_row)
    def _(j):
        pl.semaphore_signal(barrier, inc=1, device_id={"row": lax.rem(row + j, n_row)}, device_id_type=MESH)

    for load in small:
        load.wait()

    rows = block_row[...]
    owner = lax.div(rows, fine_dev)
    local = lax.rem(rows, fine_dev)
    square = (slots, slots)
    down, across = iota(square, 0), iota(square, 1)
    owner_down = jnp.sum(
        jnp.where(down == across, jnp.broadcast_to(owner, square), 0), axis=1, keepdims=True
    )
    rank = jnp.sum(jnp.where((owner_down == owner) & (down < across), 1, 0), axis=0, keepdims=True)
    owned = owner == iota((n_col, slots), 0)
    lane = iota((n_col, LANES), 1)
    padded[...] = jnp.zeros_like(padded)
    padded[:, 0:fine_dev] = bins[...]
    message = jnp.broadcast_to(padded[...], (n_col, LANES))
    for k in range(REQ):
        wanted = jnp.sum(jnp.where(owned & (rank == k), local, 0), axis=1, keepdims=True)
        message = jnp.where(lane == fine_dev + k, wanted, message)
    for c in range(n_col):
        ask[c] = message[c : c + 1, :]

    place[:, 0:slots] = owner * REQ + rank
    store_place = pltpu.make_async_copy(place, place_s, place_sem)
    store_place.start()

    paired = pair_up(block_col[...].astype(jnp.float32), slots // 2).astype(jnp.int32)
    for d in range(n_row):
        cols[d] = paired[d * cap // 2 : (d + 1) * cap // 2, :]

    lane = iota((1, 4 * LANES), 1)
    within = lax.rem(lane, LANES)
    group = lax.div(lane, LANES)
    source = jnp.where(within < half, lax.div(group, 2) * dofs + 2 * within + lax.rem(group, 2), -1)
    spread = (iota((2 * dofs, 4 * LANES), 0) == source).astype(jnp.bfloat16)
    load_res.wait()
    for q in range(CASES // 2):
        two = dot(res[:, 2 * dofs * q : 2 * dofs * (q + 1)], spread)
        for g in range(4):
            at = (g % 2) * CASES + 2 * q + g // 2
            wide[pl.ds(at, fine_dev, stride=groups), :] = two[:, g * LANES : (g + 1) * LANES]
    table[...] = wide[0 : fine_dev * groups, :].reshape(fine_dev, groups, LANES)

    pl.semaphore_wait(barrier, n_col + n_row - 2)

    def to_col(src, dst, send, recv, peer):
        return pltpu.make_async_remote_copy(
            src_ref=src, dst_ref=dst, send_sem=send, recv_sem=recv, device_id={"col": peer}, device_id_type=MESH
        )

    def to_row(src, dst, send, recv, peer):
        return pltpu.make_async_remote_copy(
            src_ref=src, dst_ref=dst, send_sem=send, recv_sem=recv, device_id={"row": peer}, device_id_type=MESH
        )

    @pl.loop(1, n_col)
    def _(j):
        peer = lax.rem(col + j, n_col)
        to_col(ask.at[peer], asked.at[col], ask_sem, ask_in, peer).start()

    asked[col] = ask[col]

    @pl.loop(1, n_row)
    def _(j):
        peer = lax.rem(row + j, n_row)
        to_row(cols.at[peer], got_cols.at[row], cols_sem, cols_in, peer).start()

    got_cols[row] = cols[row]

    wait_bytes(ask.at[pl.ds(0, n_col - 1)], ask_in)
    to_smem = pltpu.make_async_copy(asked, asked_s, asked_sem)
    to_smem.start()
    to_smem.wait()

    thirds = LANES - half
    low_lanes = iota((groups, LANES), 1) < half

    def rows_for(peer):
        picked = []
        for k in range(REQ):
            picked.append(table[asked_s[peer, 0, fine_dev + k]])
        return [
            jnp.where(low_lanes, picked[v], pltpu.roll(picked[3], half - thirds * v, 1)).astype(jnp.bfloat16)
            for v in range(3)
        ]

    @pl.loop(1, n_col)
    def _(j):
        peer = lax.rem(col + j, n_col)
        for v, tile in enumerate(rows_for(peer)):
            answer[peer, v] = tile
        to_col(answer.at[peer], got.at[pl.ds(col * REQ, 3)], answer_sem, answer_in, peer).start()

    for v, tile in enumerate(rows_for(col)):
        got[col * REQ + v] = tile

    load_blk.wait()

    @pl.loop(0, tiles, unroll=4)
    def _(t):
        at = pl.multiple_of(t * LANES, LANES)
        wide[pl.ds(t, slots, stride=tiles), :] = blk[:, pl.ds(at, LANES)].astype(jnp.float32)

    @pl.loop(0, slots)
    def _(s):
        at = pl.multiple_of(s * tiles, 8)
        packed[s, 0:half, :] = wide[pl.ds(at, half), :].astype(jnp.bfloat16)
        packed[s, half:, :] = jnp.zeros((LANES - half, LANES), jnp.bfloat16)

    all_bins = asked[...].reshape(n_col, LANES).astype(jnp.float32)
    here = (local == iota((LANES, slots), 0)).astype(jnp.float32)
    bin_of = jnp.sum(jnp.where(owned, dot(all_bins, here), 0.0), axis=0, keepdims=True).astype(jnp.int32)
    n_bins = bin_scale.shape[1]
    square = (n_bins, n_bins)
    scales = jnp.sum(
        jnp.where(iota(square, 0) == iota(square, 1), jnp.broadcast_to(bin_scale[...], square), 0.0),
        axis=1,
        keepdims=True,
    )
    scale_of = jnp.sum(jnp.where(bin_of == iota((n_bins, slots), 0), scales, 0.0), axis=0, keepdims=True)
    of_bucket = (lax.div(iota((n_row, slots), 1), cap) == iota((n_row, slots), 0)).astype(jnp.float32)
    live = lax.rem(iota((1, slots), 1), cap).astype(jnp.float32) < dot(counts[...].astype(jnp.float32), of_bucket)
    weights[...] = pair_up(jnp.where(live, scale_of, 0.0), slots // 2)

    store_place.wait()
    wait_bytes(answer.at[pl.ds(0, n_col - 1)], answer_in)

    lane_at = iota((groups, LANES), 1)

    @pl.loop(0, n_col)
    def _(c):
        a, b, d = (
            pltpu.roll(got[c * REQ + v].astype(jnp.float32), thirds * (v + 1), 1) for v in range(3)
        )
        got[c * REQ + 3] = jnp.where(
            lane_at < thirds, a, jnp.where(lane_at < 2 * thirds, b, d)
        ).astype(jnp.bfloat16)

    low = iota((CASES, LANES), 1) < LANES // 2

    def term(slot):
        panel = got[place_s[0, slot]]
        both = jnp.dot(panel, packed[slot], preferred_element_type=jnp.float32)
        return both[:CASES], both[CASES:]

    def bucket(d, dest, at):
        for pair in range(cap // 2):
            a0, a1 = term(d * cap + 2 * pair)
            b0, b1 = term(d * cap + 2 * pair + 1)
            both = jnp.where(low, a0, b1) + pltpu.roll(jnp.where(low, b0, a1), LANES // 2, 1)
            weight = weights[pl.ds(d * (cap // 2) + pair, 1), :]
            dest[at, pair * CASES : (pair + 1) * CASES, :] = both * weight

    @pl.loop(1, n_row)
    def _(j):
        peer = lax.rem(row + j, n_row)
        bucket(peer, terms, peer)
        to_row(terms.at[peer], summands.at[row], term_sem, term_in, peer).start()

    bucket(row, summands, row)

    wait_bytes(cols.at[pl.ds(0, n_row - 1)], cols_in)
    wait_bytes(terms.at[pl.ds(0, n_row - 1)], term_in)

    def add(r, sums):
        for pair in range(cap // 2):
            value = summands[r, pair * CASES : (pair + 1) * CASES, :]
            to = got_cols[r, pair : pair + 1, :]
            sums = tuple(s + jnp.where(to == a, value, 0.0) for a, s in enumerate(sums))
        return sums

    sums = lax.fori_loop(0, n_row, add, (jnp.zeros((CASES, LANES), jnp.float32),) * AG_DEV)
    for a, s in enumerate(sums):
        s = s + pltpu.roll(s, LANES // 2, 1)
        folded[a * CASES : (a + 1) * CASES, :] = jnp.where(low, s, pltpu.roll(s, CASES - 1, 0))
    for j in range(CASES // 2):
        coarse[:, j * LANES : (j + 1) * LANES] = folded[pl.ds(2 * j, AG_DEV, stride=CASES), :]

    wait_bytes(ask.at[pl.ds(0, n_col - 1)], ask_sem)
    wait_bytes(cols.at[pl.ds(0, n_row - 1)], cols_sem)
    wait_bytes(answer.at[pl.ds(0, n_col - 1)], answer_sem)
    wait_bytes(terms.at[pl.ds(0, n_row - 1)], term_sem)


def shards(n_row, n_col, residual, bins, bin_scale, blocks, block_row, block_col, counts):
    slots, entries = blocks.shape
    fine_dev, width = residual.shape
    cap = slots // n_row
    dofs = width // CASES
    aggregate = entries // dofs
    tiles = entries // LANES
    f32, bf16, i32 = jnp.float32, jnp.bfloat16, jnp.int32
    vmem = pl.BlockSpec(memory_space=pltpu.VMEM)
    hbm = pl.BlockSpec(memory_space=pltpu.HBM)
    dma = pltpu.SemaphoreType.DMA
    out = pl.pallas_call(
        functools.partial(kernel, n_row, n_col),
        out_shape=jax.ShapeDtypeStruct((AG_DEV, CASES * aggregate), f32),
        in_specs=[hbm] * 7,
        out_specs=vmem,
        scratch_shapes=[
            pltpu.VMEM((1, slots), i32),
            pltpu.VMEM((1, slots), i32),
            pltpu.VMEM((1, fine_dev), i32),
            pltpu.VMEM((1, n_row), i32),
            pltpu.VMEM((1, bin_scale.shape[0]), f32),
            pltpu.VMEM((1, LANES), i32),
            pltpu.VMEM((fine_dev, width), bf16),
            pltpu.VMEM((slots, entries), bf16),
            pltpu.VMEM((slots * tiles, LANES), f32),
            pltpu.VMEM((slots, LANES, LANES), bf16),
            pltpu.VMEM((fine_dev, 2 * CASES, LANES), f32),
            pltpu.VMEM((n_col, 1, LANES), i32),
            pltpu.VMEM((n_col, 1, LANES), i32),
            pltpu.SMEM((n_col, 1, LANES), i32),
            pltpu.VMEM((1, LANES), i32),
            pltpu.SMEM((1, LANES), i32),
            pltpu.VMEM((n_col, 3, 2 * CASES, LANES), bf16),
            pltpu.VMEM((n_col * REQ, 2 * CASES, LANES), bf16),
            pltpu.VMEM((n_row, cap // 2 * CASES, LANES), f32),
            pltpu.VMEM((n_row, cap // 2 * CASES, LANES), f32),
            pltpu.VMEM((n_row, cap // 2, LANES), i32),
            pltpu.VMEM((n_row, cap // 2, LANES), i32),
            pltpu.VMEM((slots // 2, LANES), f32),
            pltpu.VMEM((AG_DEV * CASES, LANES), f32),
            dma((7,)),
        ]
        + [dma] * 10,
        compiler_params=pltpu.CompilerParams(
            collective_id=0, has_side_effects=True, vmem_limit_bytes=60 * 1024 * 1024
        ),
    )(
        residual,
        blocks,
        block_row.reshape(1, -1),
        block_col.reshape(1, -1),
        bins.reshape(1, -1),
        counts.reshape(1, -1),
        bin_scale.reshape(1, -1),
    )
    return out[None]


def solution(mesh):
    both = P(("row", "col"))
    rows = P(("row", "col"), None)
    return jax.shard_map(
        functools.partial(shards, mesh.shape["row"], mesh.shape["col"]),
        mesh=mesh,
        in_specs=(rows, both, P(), rows, both, both, both),
        out_specs=P("col", "row", None),
        check_vma=False,
    )
```

time: 221 us -> 47.2 us (0.21)
  waiting for transfers between devices: 122 us -> 0 us
  Pallas kernels: 0 us -> 45.7 us
  starting transfers between devices: 43.9 us -> 0 us
  blocking collectives: 17.6 us -> 0 us
  local copies, waits for them, and re-layouts: 16.7 us -> 1.32 us
  between operations: 14.1 us -> 0.01 us
  other arithmetic: 3.55 us -> 0 us
  matrix products: 2.44 us -> 0 us
    all_gather x1 -> x0, waiting for transfers between devices: 112 us -> none  [shards(): lax.all_gather(residual, 'col', axis=0, tiled=True)]
    pallas_call x0 -> x1, Pallas kernels: none -> 45.7 us  [shards(): pl.pallas_call(functools.partial(kernel, n_row, n_col), out_shape=jax.Sha...]
    all_to_all x2 -> x0, starting transfers between devices: 43.9 us -> none  [the longest x1 29.6 us: shards(): lax.all_to_all(terms, 'row', split_axis=0, concat_axis=0, tiled=True)]
    unnamed x1 -> x0, blocking collectives: 17.6 us -> none
    all_to_all x2 -> x0, waiting for transfers between devices: 8.78 us -> none  [the longest x1 8.78 us: shards(): lax.all_to_all(terms, 'row', split_axis=0, concat_axis=0, tiled=True)]
    gather x3 -> x0, local copies, waits for them, and re-layouts: 7.1 us -> none  [the longest x2 6.33 us: shards(): panels = jnp.take(whole, block_row, axis=0)]
    reshape x2 -> x0, local copies, waits for them, and re-layouts: 5.41 us -> none  [the longest x1 4.33 us: products(): block_view = blocks.reshape(count, fine_dofs, width // fine_dofs)]
    dot_general x2 -> x0, matrix products: 2.44 us -> none  [the longest x1 1.67 us: products(): jnp.einsum('ncf,nfa->nca', panel_view, block_view, preferred_element_type...]
  transfers between devices with their start and end apart: 3 -> 0, of which waited for: 2 -> 0; matrix products, arithmetic and copies ran while one was open for 9% -> 0% of each run, Pallas kernels for 0% -> 0%
where the time goes in v1:
time: 47.2 us; the launch traced here: 47 us
  Pallas kernels  45.7 us (97%)
  local copies, waits for them, and re-layouts  1.32 us (3%)
    pallas_call x1, Pallas kernels, shards(): pl.pallas_call(functools.partial(kernel, n_row, n_col), out_shape=jax.Sha...  45.7 us
    unnamed x1, local copies, waits for them, and re-layouts  1.32 us

profile of v1, /device:TPU:1, one launch (start us, length us, event | category | flops | bytes accessed | tf_op | source)
XLA Modules:
  0.0 47.0 jit_solution(18205951446100342839)
XLA Ops:
  0.0 45.7 %shard_map.73 = f32[8,512]{1,0:T(8,128)} custom-call(bf16[64,1536]{1,0:T(8,128)(2,1)} %residual.1, bf16[64,12288]{1,0:T(8,128)(2,1)} %blocks.1, s32[1,64]{1,0:T(1,128)} %bitcast.7, s32[1,64]{1,0:T(1,128)} %bitcast.8, s32[1,64]{1,0:T(1,128)} %bitcast.9, s32[1,16]{1,0:T(1,128)} %bitcast.10, f32[1,16]{1,0:T(1,128)} %bitcast.11), custom_call_target="tpu_custom_call" | custom-call | tf_op jit(solution)/shard_map/pallas_call | solution.py:324
  45.7 1.3 %copy.9 = f32[1,8,512]{2,1,0:T(8,128)} copy(f32[1,8,512]{2,1,0:T(8,128)} %bitcast.6) | data formatting | bytes 32768

commit v2 on v1

--- a/solution.py
+++ b/solution.py
@@ -11,6 +11,7 @@
 AG_DEV = 8
 REQ = 4
 LANES = 128
+RUN = 4
 MESH = pl.DeviceIdType.MESH
 
 
@@ -96,6 +97,39 @@
     groups = 2 * CASES
     tiles = blk.shape[1] // LANES
 
+    n_z = min(RUN, n_col)
+    n_y = n_col // n_z
+
+    def col_peer(group, i):
+        far = n_y - 1 - group
+        step = lax.div(far + 1, 2) * (2 * lax.rem(far, 2) - 1)
+        y = lax.rem(lax.div(col, n_z) + n_y // 2 + step + n_y, n_y)
+        return y * n_z + lax.rem(lax.rem(col, n_z) + i + 1, n_z)
+
+    halves = n_row // 2
+
+    def row_peer(t):
+        near = lax.div(t, halves)
+        half_of = lax.rem(lax.div(row, halves) + 1 - near, 2)
+        return half_of * halves + lax.rem(lax.rem(row, halves) + lax.rem(t, halves) + near, halves)
+
+    barrier = pltpu.get_barrier_semaphore()
+
+    def greet_col(group, i):
+        pl.semaphore_signal(barrier, inc=1, device_id={"col": col_peer(group, i)}, device_id_type=MESH)
+
+    @pl.loop(0, n_y - 1)
+    def _(g):
+        for i in range(n_z):
+            greet_col(n_y - 1 - g, i)
+
+    @pl.loop(0, n_row - 1)
+    def _(t):
+        pl.semaphore_signal(barrier, inc=1, device_id={"row": row_peer(t)}, device_id_type=MESH)
+
+    for i in range(n_z - 1):
+        greet_col(0, i)
+
     small = [
         pltpu.make_async_copy(a, b, load_sem.at[2 + i])
         for i, (a, b) in enumerate(
@@ -114,17 +148,6 @@
     load_res.start()
     load_blk = pltpu.make_async_copy(blocks, blk, load_sem.at[1])
     load_blk.start()
-
-    barrier = pltpu.get_barrier_semaphore()
-
-    @pl.loop(1, n_col)
-    def _(j):
-        pl.semaphore_signal(barrier, inc=1, device_id={"col": lax.rem(col + j, n_col)}, device_id_type=MESH)
-
-    @pl.loop(1, n_row)
-    def _(j):
-        pl.semaphore_signal(barrier, inc=1, device_id={"row": lax.rem(row + j, n_row)}, device_id_type=MESH)
-
     for load in small:
         load.wait()
 
@@ -181,24 +204,39 @@
             src_ref=src, dst_ref=dst, send_sem=send, recv_sem=recv, device_id={"row": peer}, device_id_type=MESH
         )
 
-    @pl.loop(1, n_col)
-    def _(j):
-        peer = lax.rem(col + j, n_col)
-        to_col(ask.at[peer], asked.at[col], ask_sem, ask_in, peer).start()
+    def request(group, i):
+        peer = col_peer(group, i)
+        to_col(ask.at[peer], asked.at[col], ask_sem, ask_in.at[col], peer).start()
+
+    @pl.loop(0, n_y - 1)
+    def _(g):
+        for i in range(n_z):
+            request(n_y - 1 - g, i)
+
+    for i in range(n_z - 1):
+        request(0, i)
 
     asked[col] = ask[col]
 
-    @pl.loop(1, n_row)
-    def _(j):
-        peer = lax.rem(row + j, n_row)
-        to_row(cols.at[peer], got_cols.at[row], cols_sem, cols_in, peer).start()
+    @pl.loop(0, n_row - 1)
+    def _(t):
+        peer = row_peer(t)
+        to_row(cols.at[peer], got_cols.at[row], cols_sem, cols_in.at[row], peer).start()
 
     got_cols[row] = cols[row]
 
-    wait_bytes(ask.at[pl.ds(0, n_col - 1)], ask_in)
-    to_smem = pltpu.make_async_copy(asked, asked_s, asked_sem)
-    to_smem.start()
-    to_smem.wait()
+    load_blk.wait()
+
+    @pl.loop(0, tiles, unroll=4)
+    def _(t):
+        at = pl.multiple_of(t * LANES, LANES)
+        wide[pl.ds(t, slots, stride=tiles), :] = blk[:, pl.ds(at, LANES)].astype(jnp.float32)
+
+    @pl.loop(0, slots)
+    def _(s):
+        at = pl.multiple_of(s * tiles, 8)
+        packed[s, 0:half, :] = wide[pl.ds(at, half), :].astype(jnp.bfloat16)
+        packed[s, half:, :] = jnp.zeros((LANES - half, LANES), jnp.bfloat16)
 
     thirds = LANES - half
     low_lanes = iota((groups, LANES), 1) < half
@@ -212,28 +250,40 @@
             for v in range(3)
         ]
 
-    @pl.loop(1, n_col)
-    def _(j):
-        peer = lax.rem(col + j, n_col)
-        for v, tile in enumerate(rows_for(peer)):
-            answer[peer, v] = tile
-        to_col(answer.at[peer], got.at[pl.ds(col * REQ, 3)], answer_sem, answer_in, peer).start()
-
-    for v, tile in enumerate(rows_for(col)):
-        got[col * REQ + v] = tile
-
-    load_blk.wait()
-
-    @pl.loop(0, tiles, unroll=4)
-    def _(t):
-        at = pl.multiple_of(t * LANES, LANES)
-        wide[pl.ds(t, slots, stride=tiles), :] = blk[:, pl.ds(at, LANES)].astype(jnp.float32)
-
-    @pl.loop(0, slots)
-    def _(s):
-        at = pl.multiple_of(s * tiles, 8)
-        packed[s, 0:half, :] = wide[pl.ds(at, half), :].astype(jnp.bfloat16)
-        packed[s, half:, :] = jnp.zeros((LANES - half, LANES), jnp.bfloat16)
+    def take(group, count):
+        peers = [col_peer(group, i) for i in range(n_z)]
+        for peer in peers[:count]:
+            wait_bytes(asked.at[peer], ask_in.at[peer])
+        for peer in peers:
+            pltpu.make_async_copy(asked.at[peer], asked_s.at[peer], asked_sem.at[peer]).start()
+
+    def reply(group, count):
+        peers = [col_peer(group, i) for i in range(n_z)]
+        for peer in peers:
+            pltpu.make_async_copy(asked.at[peer], asked_s.at[peer], asked_sem.at[peer]).wait()
+        filled = [rows_for(peer) for peer in peers]
+        for peer, rows_of in zip(peers[:count], filled):
+            for v, tile in enumerate(rows_of):
+                answer[peer, v] = tile
+            to_col(
+                answer.at[peer], got.at[pl.ds(col * REQ, 3)], answer_sem, answer_in.at[col], peer
+            ).start()
+        if count < n_z:
+            for v, tile in enumerate(filled[-1]):
+                got[col * REQ + v] = tile
+
+    take(0, n_z - 1)
+    if n_y > 1:
+        take(1, n_z)
+    reply(0, n_z - 1)
+
+    @pl.loop(2, n_y)
+    def _(g):
+        take(g, n_z)
+        reply(g - 1, n_z)
+
+    if n_y > 1:
+        reply(n_y - 1, n_z)
 
     all_bins = asked[...].reshape(n_col, LANES).astype(jnp.float32)
     here = (local == iota((LANES, slots), 0)).astype(jnp.float32)
@@ -251,18 +301,26 @@
     weights[...] = pair_up(jnp.where(live, scale_of, 0.0), slots // 2)
 
     store_place.wait()
-    wait_bytes(answer.at[pl.ds(0, n_col - 1)], answer_in)
-
     lane_at = iota((groups, LANES), 1)
 
-    @pl.loop(0, n_col)
-    def _(c):
-        a, b, d = (
-            pltpu.roll(got[c * REQ + v].astype(jnp.float32), thirds * (v + 1), 1) for v in range(3)
-        )
-        got[c * REQ + 3] = jnp.where(
-            lane_at < thirds, a, jnp.where(lane_at < 2 * thirds, b, d)
-        ).astype(jnp.bfloat16)
+    def gather_thirds(group, count):
+        peers = [col_peer(group, i) for i in range(n_z)]
+        for peer in peers[:count]:
+            wait_bytes(got.at[pl.ds(peer * REQ, 3)], answer_in.at[peer])
+        joined = []
+        for peer in peers:
+            a, b, d = (
+                pltpu.roll(got[peer * REQ + v].astype(jnp.float32), thirds * (v + 1), 1) for v in range(3)
+            )
+            joined.append(jnp.where(lane_at < thirds, a, jnp.where(lane_at < 2 * thirds, b, d)))
+        for peer, tile in zip(peers, joined):
+            got[peer * REQ + 3] = tile.astype(jnp.bfloat16)
+
+    gather_thirds(0, n_z - 1)
+
+    @pl.loop(1, n_y)
+    def _(g):
+        gather_thirds(g, n_z)
 
     low = iota((CASES, LANES), 1) < LANES // 2
 
@@ -271,24 +329,35 @@
         both = jnp.dot(panel, packed[slot], preferred_element_type=jnp.float32)
         return both[:CASES], both[CASES:]
 
-    def bucket(d, dest, at):
+    def bucket(d):
+        pairs = []
         for pair in range(cap // 2):
             a0, a1 = term(d * cap + 2 * pair)
             b0, b1 = term(d * cap + 2 * pair + 1)
             both = jnp.where(low, a0, b1) + pltpu.roll(jnp.where(low, b0, a1), LANES // 2, 1)
-            weight = weights[pl.ds(d * (cap // 2) + pair, 1), :]
-            dest[at, pair * CASES : (pair + 1) * CASES, :] = both * weight
-
-    @pl.loop(1, n_row)
-    def _(j):
-        peer = lax.rem(row + j, n_row)
-        bucket(peer, terms, peer)
-        to_row(terms.at[peer], summands.at[row], term_sem, term_in, peer).start()
-
-    bucket(row, summands, row)
-
-    wait_bytes(cols.at[pl.ds(0, n_row - 1)], cols_in)
-    wait_bytes(terms.at[pl.ds(0, n_row - 1)], term_in)
+            pairs.append(both * weights[pl.ds(d * (cap // 2) + pair, 1), :])
+        return pairs
+
+    def store(dest, at, pairs):
+        for pair, value in enumerate(pairs):
+            dest[at, pair * CASES : (pair + 1) * CASES, :] = value
+
+    def send(peers, summed):
+        for peer, pairs in zip(peers, summed):
+            store(terms, peer, pairs)
+            to_row(terms.at[peer], summands.at[row], term_sem, term_in.at[row], peer).start()
+
+    together = min(4, n_row)
+
+    @pl.loop(0, n_row // together - 1)
+    def _(g):
+        peers = [row_peer(g * together + i) for i in range(together)]
+        send(peers, [bucket(d) for d in peers])
+
+    peers = [row_peer(n_row - together + i) for i in range(together - 1)]
+    summed = [bucket(d) for d in peers + [row]]
+    send(peers, summed[:-1])
+    store(summands, row, summed[-1])
 
     def add(r, sums):
         for pair in range(cap // 2):
@@ -297,7 +366,14 @@
             sums = tuple(s + jnp.where(to == a, value, 0.0) for a, s in enumerate(sums))
         return sums
 
-    sums = lax.fori_loop(0, n_row, add, (jnp.zeros((CASES, LANES), jnp.float32),) * AG_DEV)
+    def arrive(t, sums):
+        peer = row_peer(n_row - 2 - t)
+        wait_bytes(got_cols.at[peer], cols_in.at[peer])
+        wait_bytes(summands.at[peer], term_in.at[peer])
+        return add(peer, sums)
+
+    sums = add(row, (jnp.zeros((CASES, LANES), jnp.float32),) * AG_DEV)
+    sums = lax.fori_loop(0, n_row - 1, arrive, sums)
     for a, s in enumerate(sums):
         s = s + pltpu.roll(s, LANES // 2, 1)
         folded[a * CASES : (a + 1) * CASES, :] = jnp.where(low, s, pltpu.roll(s, CASES - 1, 0))
@@ -353,7 +429,8 @@
             pltpu.VMEM((AG_DEV * CASES, LANES), f32),
             dma((7,)),
         ]
-        + [dma] * 10,
+        + [dma, dma, dma((n_col,)), dma((n_col,)), dma, dma((n_col,))]
+        + [dma, dma((n_row,)), dma, dma((n_row,))],
         compiler_params=pltpu.CompilerParams(
             collective_id=0, has_side_effects=True, vmem_limit_bytes=60 * 1024 * 1024
         ),

time: 47.2 us -> 43.5 us (0.922)
  Pallas kernels: 45.7 us -> 42 us
    pallas_call x1, Pallas kernels: 45.7 us -> 42 us  [shards(): pl.pallas_call(functools.partial(kernel, n_row, n_col), out_shape=jax.Sha...]
where the time goes in v2:
time: 43.5 us; the launch traced here: 43.3 us
  Pallas kernels  42 us (97%)
  local copies, waits for them, and re-layouts  1.32 us (3%)
    pallas_call x1, Pallas kernels, shards(): pl.pallas_call(functools.partial(kernel, n_row, n_col), out_shape=jax.Sha...  42 us
    unnamed x1, local copies, waits for them, and re-layouts  1.32 us

profile of v2, /device:TPU:1, one launch (start us, length us, event | category | flops | bytes accessed | tf_op | source)
XLA Modules:
  0.0 43.3 jit_solution(15241367884368221329)
XLA Ops:
  0.0 42.0 %shard_map.73 = f32[8,512]{1,0:T(8,128)} custom-call(bf16[64,1536]{1,0:T(8,128)(2,1)} %residual.1, bf16[64,12288]{1,0:T(8,128)(2,1)} %blocks.1, s32[1,64]{1,0:T(1,128)} %bitcast.7, s32[1,64]{1,0:T(1,128)} %bitcast.8, s32[1,64]{1,0:T(1,128)} %bitcast.9, s32[1,16]{1,0:T(1,128)} %bitcast.10, f32[1,16]{1,0:T(1,128)} %bitcast.11), custom_call_target="tpu_custom_call" | custom-call | tf_op jit(solution)/shard_map/pallas_call | solution.py:400
  42.0 1.3 %copy.9 = f32[1,8,512]{2,1,0:T(8,128)} copy(f32[1,8,512]{2,1,0:T(8,128)} %bitcast.6) | data formatting | bytes 32768

commit v3 on v2

--- a/solution.py
+++ b/solution.py
@@ -65,7 +65,6 @@
     table,
     ask,
     asked,
-    asked_s,
     place,
     place_s,
     answer,
@@ -80,7 +79,6 @@
     place_sem,
     ask_sem,
     ask_in,
-    asked_sem,
     answer_sem,
     answer_in,
     term_sem,
@@ -225,26 +223,13 @@
 
     got_cols[row] = cols[row]
 
-    load_blk.wait()
-
-    @pl.loop(0, tiles, unroll=4)
-    def _(t):
-        at = pl.multiple_of(t * LANES, LANES)
-        wide[pl.ds(t, slots, stride=tiles), :] = blk[:, pl.ds(at, LANES)].astype(jnp.float32)
-
-    @pl.loop(0, slots)
-    def _(s):
-        at = pl.multiple_of(s * tiles, 8)
-        packed[s, 0:half, :] = wide[pl.ds(at, half), :].astype(jnp.bfloat16)
-        packed[s, half:, :] = jnp.zeros((LANES - half, LANES), jnp.bfloat16)
-
     thirds = LANES - half
     low_lanes = iota((groups, LANES), 1) < half
 
     def rows_for(peer):
         picked = []
         for k in range(REQ):
-            picked.append(table[asked_s[peer, 0, fine_dev + k]])
+            picked.append(table[asked[peer, 0, fine_dev + k]])
         return [
             jnp.where(low_lanes, picked[v], pltpu.roll(picked[3], half - thirds * v, 1)).astype(jnp.bfloat16)
             for v in range(3)
@@ -254,13 +239,9 @@
         peers = [col_peer(group, i) for i in range(n_z)]
         for peer in peers[:count]:
             wait_bytes(asked.at[peer], ask_in.at[peer])
-        for peer in peers:
-            pltpu.make_async_copy(asked.at[peer], asked_s.at[peer], asked_sem.at[peer]).start()
 
     def reply(group, count):
         peers = [col_peer(group, i) for i in range(n_z)]
-        for peer in peers:
-            pltpu.make_async_copy(asked.at[peer], asked_s.at[peer], asked_sem.at[peer]).wait()
         filled = [rows_for(peer) for peer in peers]
         for peer, rows_of in zip(peers[:count], filled):
             for v, tile in enumerate(rows_of):
@@ -273,17 +254,25 @@
                 got[col * REQ + v] = tile
 
     take(0, n_z - 1)
-    if n_y > 1:
-        take(1, n_z)
     reply(0, n_z - 1)
 
-    @pl.loop(2, n_y)
+    @pl.loop(1, n_y)
     def _(g):
         take(g, n_z)
-        reply(g - 1, n_z)
-
-    if n_y > 1:
-        reply(n_y - 1, n_z)
+        reply(g, n_z)
+
+    load_blk.wait()
+
+    @pl.loop(0, tiles, unroll=4)
+    def _(t):
+        at = pl.multiple_of(t * LANES, LANES)
+        wide[pl.ds(t, slots, stride=tiles), :] = blk[:, pl.ds(at, LANES)].astype(jnp.float32)
+
+    @pl.loop(0, slots)
+    def _(s):
+        at = pl.multiple_of(s * tiles, 8)
+        packed[s, 0:half, :] = wide[pl.ds(at, half), :].astype(jnp.bfloat16)
+        packed[s, half:, :] = jnp.zeros((LANES - half, LANES), jnp.bfloat16)
 
     all_bins = asked[...].reshape(n_col, LANES).astype(jnp.float32)
     here = (local == iota((LANES, slots), 0)).astype(jnp.float32)
@@ -416,7 +405,6 @@
             pltpu.VMEM((fine_dev, 2 * CASES, LANES), f32),
             pltpu.VMEM((n_col, 1, LANES), i32),
             pltpu.VMEM((n_col, 1, LANES), i32),
-            pltpu.SMEM((n_col, 1, LANES), i32),
             pltpu.VMEM((1, LANES), i32),
             pltpu.SMEM((1, LANES), i32),
             pltpu.VMEM((n_col, 3, 2 * CASES, LANES), bf16),
@@ -429,19 +417,24 @@
             pltpu.VMEM((AG_DEV * CASES, LANES), f32),
             dma((7,)),
         ]
-        + [dma, dma, dma((n_col,)), dma((n_col,)), dma, dma((n_col,))]
+        + [dma, dma, dma((n_col,)), dma, dma((n_col,))]
         + [dma, dma((n_row,)), dma, dma((n_row,))],
         compiler_params=pltpu.CompilerParams(
-            collective_id=0, has_side_effects=True, vmem_limit_bytes=60 * 1024 * 1024
+            collective_id=0, has_side_effects=True, vmem_limit_bytes=32 * 1024 * 1024
         ),
     )(
-        residual,
-        blocks,
-        block_row.reshape(1, -1),
-        block_col.reshape(1, -1),
-        bins.reshape(1, -1),
-        counts.reshape(1, -1),
-        bin_scale.reshape(1, -1),
+        *(
+            pltpu.with_memory_space_constraint(a, pltpu.HBM)
+            for a in (
+                residual,
+                blocks,
+                block_row.reshape(1, -1),
+                block_col.reshape(1, -1),
+                bins.reshape(1, -1),
+                counts.reshape(1, -1),
+                bin_scale.reshape(1, -1),
+            )
+        )
     )
     return out[None]
 

time: 43.5 us -> 40 us (0.920)
  Pallas kernels: 42 us -> 39.1 us
  local copies, waits for them, and re-layouts: 1.32 us -> 0.61 us
    pallas_call x1, Pallas kernels: 42 us -> 39.1 us  [shards(): pl.pallas_call(functools.partial(kernel, n_row, n_col), out_shape=jax.Sha...]
    unnamed x1, local copies, waits for them, and re-layouts: 1.32 us -> 0.61 us
where the time goes in v3:
time: 40 us; the launch traced here: 39.7 us
  Pallas kernels  39.1 us (98%)
  local copies, waits for them, and re-layouts  0.61 us (2%)
    pallas_call x1, Pallas kernels, shards(): pl.pallas_call(functools.partial(kernel, n_row, n_col), out_shape=jax.Sha...  39.1 us

profile of v3, /device:TPU:1, one launch (start us, length us, event | category | flops | bytes accessed | tf_op | source)
XLA Modules:
  0.0 39.7 jit_solution(12786397614069870817)
XLA Ops:
  0.0 39.1 %shard_map.73 = f32[8,512]{1,0:T(8,128)S(1)} custom-call(bf16[64,1536]{1,0:T(8,128)(2,1)} %residual.1, bf16[64,12288]{1,0:T(8,128)(2,1)} %blocks.1, s32[1,64]{1,0:T(1,128)} %bitcast.7, s32[1,64]{1,0:T(1,128)} %bitcast.8, s32[1,64]{1,0:T(1,128)} %bitcast.9, s32[1,16]{1,0:T(1,128)} %bitcast.10, f32[1,16]{1,0:T(1,128)} %bitcast.11), custom_call_target="tpu_custom_call" | custom-call | tf_op jit(solution)/shard_map/pallas_call | solution.py:389
  39.1 0.6 %copy.9 = f32[1,8,512]{2,1,0:T(8,128)} copy(f32[1,8,512]{2,1,0:T(8,128)S(1)} %bitcast.6) | data formatting | bytes 32768

commit v4 on v3

--- a/solution.py
+++ b/solution.py
@@ -116,14 +116,25 @@
     def greet_col(group, i):
         pl.semaphore_signal(barrier, inc=1, device_id={"col": col_peer(group, i)}, device_id_type=MESH)
 
-    @pl.loop(0, n_y - 1)
+    def greet_row(t):
+        pl.semaphore_signal(barrier, inc=1, device_id={"row": row_peer(t)}, device_id_type=MESH)
+
+    if n_y > 1:
+        for i in range(n_z):
+            greet_col(n_y - 1, i)
+
+    @pl.loop(0, halves)
+    def _(t):
+        greet_row(t)
+
+    @pl.loop(1, n_y - 1)
     def _(g):
         for i in range(n_z):
             greet_col(n_y - 1 - g, i)
 
-    @pl.loop(0, n_row - 1)
+    @pl.loop(halves, n_row - 1)
     def _(t):
-        pl.semaphore_signal(barrier, inc=1, device_id={"row": row_peer(t)}, device_id_type=MESH)
+        greet_row(t)
 
     for i in range(n_z - 1):
         greet_col(0, i)
@@ -266,12 +277,11 @@
     @pl.loop(0, tiles, unroll=4)
     def _(t):
         at = pl.multiple_of(t * LANES, LANES)
-        wide[pl.ds(t, slots, stride=tiles), :] = blk[:, pl.ds(at, LANES)].astype(jnp.float32)
+        wide[pl.ds(t, slots, stride=tiles + 1), :] = blk[:, pl.ds(at, LANES)].astype(jnp.float32)
 
     @pl.loop(0, slots)
     def _(s):
-        at = pl.multiple_of(s * tiles, 8)
-        packed[s, 0:half, :] = wide[pl.ds(at, half), :].astype(jnp.bfloat16)
+        packed[s, 0:half, :] = wide[pl.ds(s * (tiles + 1), half), :].astype(jnp.bfloat16)
         packed[s, half:, :] = jnp.zeros((LANES - half, LANES), jnp.bfloat16)
 
     all_bins = asked[...].reshape(n_col, LANES).astype(jnp.float32)
@@ -355,14 +365,24 @@
             sums = tuple(s + jnp.where(to == a, value, 0.0) for a, s in enumerate(sums))
         return sums
 
-    def arrive(t, sums):
-        peer = row_peer(n_row - 2 - t)
+    @pl.loop(0, n_row - 1)
+    def _(t):
+        peer = row_peer(t)
         wait_bytes(got_cols.at[peer], cols_in.at[peer])
-        wait_bytes(summands.at[peer], term_in.at[peer])
-        return add(peer, sums)
+
+    def arrive(peers, sums):
+        for peer in peers:
+            wait_bytes(summands.at[peer], term_in.at[peer])
+        for peer in peers:
+            sums = add(peer, sums)
+        return sums
+
+    def group_of(g):
+        return [row_peer(n_row - 1 - g * together - i) for i in range(together)]
 
     sums = add(row, (jnp.zeros((CASES, LANES), jnp.float32),) * AG_DEV)
-    sums = lax.fori_loop(0, n_row - 1, arrive, sums)
+    sums = arrive(group_of(0)[1:], sums)
+    sums = lax.fori_loop(1, n_row // together, lambda g, sums: arrive(group_of(g), sums), sums)
     for a, s in enumerate(sums):
         s = s + pltpu.roll(s, LANES // 2, 1)
         folded[a * CASES : (a + 1) * CASES, :] = jnp.where(low, s, pltpu.roll(s, CASES - 1, 0))
@@ -400,7 +420,7 @@
             pltpu.VMEM((1, LANES), i32),
             pltpu.VMEM((fine_dev, width), bf16),
             pltpu.VMEM((slots, entries), bf16),
-            pltpu.VMEM((slots * tiles, LANES), f32),
+            pltpu.VMEM(((slots + 1) * (tiles + 1), LANES), f32),
             pltpu.VMEM((slots, LANES, LANES), bf16),
             pltpu.VMEM((fine_dev, 2 * CASES, LANES), f32),
             pltpu.VMEM((n_col, 1, LANES), i32),
@@ -414,7 +434,7 @@
             pltpu.VMEM((n_row, cap // 2, LANES), i32),
             pltpu.VMEM((n_row, cap // 2, LANES), i32),
             pltpu.VMEM((slots // 2, LANES), f32),
-            pltpu.VMEM((AG_DEV * CASES, LANES), f32),
+            pltpu.VMEM(((AG_DEV + 1) * CASES, LANES), f32),
             dma((7,)),
         ]
         + [dma, dma, dma((n_col,)), dma, dma((n_col,))]

time: 40 us -> 40.1 us (level)
  no operation moved by 1% of the time
where the time goes in v4:
time: 40.1 us; the launch traced here: 39.7 us
  Pallas kernels  39.1 us (98%)
  local copies, waits for them, and re-layouts  0.61 us (2%)
    pallas_call x1, Pallas kernels, shards(): pl.pallas_call(functools.partial(kernel, n_row, n_col), out_shape=jax.Sha...  39.1 us

profile of v4, /device:TPU:1, one launch (start us, length us, event | category | flops | bytes accessed | tf_op | source)
XLA Modules:
  0.0 39.7 jit_solution(8204323166863276836)
XLA Ops:
  0.0 39.1 %shard_map.73 = f32[8,512]{1,0:T(8,128)S(1)} custom-call(bf16[64,1536]{1,0:T(8,128)(2,1)} %residual.1, bf16[64,12288]{1,0:T(8,128)(2,1)} %blocks.1, s32[1,64]{1,0:T(1,128)} %bitcast.7, s32[1,64]{1,0:T(1,128)} %bitcast.8, s32[1,64]{1,0:T(1,128)} %bitcast.9, s32[1,16]{1,0:T(1,128)} %bitcast.10, f32[1,16]{1,0:T(1,128)} %bitcast.11), custom_call_target="tpu_custom_call" | custom-call | tf_op jit(solution)/shard_map/pallas_call | solution.py:409
  39.1 0.6 %copy.9 = f32[1,8,512]{2,1,0:T(8,128)} copy(f32[1,8,512]{2,1,0:T(8,128)S(1)} %bitcast.6) | data formatting | bytes 32768

commit v5 on v4

--- a/solution.py
+++ b/solution.py
@@ -109,7 +109,8 @@
     def row_peer(t):
         near = lax.div(t, halves)
         half_of = lax.rem(lax.div(row, halves) + 1 - near, 2)
-        return half_of * halves + lax.rem(lax.rem(row, halves) + lax.rem(t, halves) + near, halves)
+        ahead = near + (1 - near) * max(halves // 2 - 1, 0)
+        return half_of * halves + lax.rem(lax.rem(row, halves) + lax.rem(t, halves) + ahead, halves)
 
     barrier = pltpu.get_barrier_semaphore()
 

time: 40.1 us -> 39.9 us (level)
  no operation moved by 1% of the time
where the time goes in v5:
time: 39.9 us; the launch traced here: 39.5 us
  Pallas kernels  38.9 us (97%)
  local copies, waits for them, and re-layouts  0.61 us (2%)
    pallas_call x1, Pallas kernels, shards(): pl.pallas_call(functools.partial(kernel, n_row, n_col), out_shape=jax.Sha...  38.9 us

profile of v5, /device:TPU:1, one launch (start us, length us, event | category | flops | bytes accessed | tf_op | source)
XLA Modules:
  0.0 39.5 jit_solution(3984559961225829329)
XLA Ops:
  0.0 38.9 %shard_map.73 = f32[8,512]{1,0:T(8,128)S(1)} custom-call(bf16[64,1536]{1,0:T(8,128)(2,1)} %residual.1, bf16[64,12288]{1,0:T(8,128)(2,1)} %blocks.1, s32[1,64]{1,0:T(1,128)} %bitcast.7, s32[1,64]{1,0:T(1,128)} %bitcast.8, s32[1,64]{1,0:T(1,128)} %bitcast.9, s32[1,16]{1,0:T(1,128)} %bitcast.10, f32[1,16]{1,0:T(1,128)} %bitcast.11), custom_call_target="tpu_custom_call" | custom-call | tf_op jit(solution)/shard_map/pallas_call | solution.py:410
  38.9 0.6 %copy.9 = f32[1,8,512]{2,1,0:T(8,128)} copy(f32[1,8,512]{2,1,0:T(8,128)S(1)} %bitcast.6) | data formatting | bytes 32768
